TPU v7x, 128 devices: a whole 4x4x4 slice. The times are simulated.
128 devices in a mesh: wide: 32 (over y, z, x_lo), narrow: 4 (over x_hi, core).
Axes of the slice: x: 4 (x_hi: 2, x_lo: 2; x = x_hi * 2 + x_lo), y: 4, z: 4, core: 2. Of those that a mesh axis runs over, the one named last changes fastest.
Arguments:
- target_hidden: bfloat16 [512, 16384], P(('wide', 'narrow'))
- target_weight: bfloat16 [16384, 65536], P(None, ('wide', 'narrow')), may hold values from -0.046875 to 0.046875
- draft_hidden: bfloat16 [512, 4096], P(('wide', 'narrow'))
- draft_weight: bfloat16 [4096, 65536], P(None, ('wide', 'narrow')), may hold values from -0.09375 to 0.09375
- draft_tokens: int32 [512], replicated, may hold values from 0 to 65535
Outputs:
- target_logprob: float32 [512, 65536], P(None, ('wide', 'narrow'))
- draft_logprob: float32 [512, 65536], P(None, ('wide', 'narrow'))
- residual: float32 [512, 65536], P(None, ('wide', 'narrow'))
- acceptance: float32 [512], replicated
- leftover: float32 [512], replicated
All inputs are finite; a program needn't handle non-finite values.
Results may differ from a plain program's by a relative error of at most 0.0011.
Values may be sent and summed in bfloat16 or wider, within the bound.
A program may use at most 128 MiB of HBM per device.

v0:
```python
import jax
import jax.numpy as jnp
from jax import lax
from jax.sharding import PartitionSpec as P


def on_device(target_hidden, target_weight, draft_hidden, draft_weight, draft_tokens):
    columns_dev = target_weight.shape[1]
    offset = lax.axis_index(("wide", "narrow")) * columns_dev
    target_logits = jnp.dot(
        lax.all_gather(target_hidden, ("wide", "narrow"), axis=0, tiled=True),
        target_weight,
        preferred_element_type=jnp.float32,
    )
    draft_logits = jnp.dot(
        lax.all_gather(draft_hidden, ("wide", "narrow"), axis=0, tiled=True),
        draft_weight,
        preferred_element_type=jnp.float32,
    )
    vocab_ids = offset + jnp.arange(columns_dev, dtype=jnp.int32)
    picked = draft_tokens[:, None] == vocab_ids[None, :]
    target_sel = jnp.sum(jnp.where(picked, target_logits, 0.0), axis=1)
    draft_sel = jnp.sum(jnp.where(picked, draft_logits, 0.0), axis=1)
    target_top = jnp.max(target_logits, axis=1)
    draft_top = jnp.max(draft_logits, axis=1)
    target_max, draft_max = lax.pmax((target_top, draft_top), ("wide", "narrow"))
    target_local = jnp.sum(jnp.exp(target_logits - target_max[:, None]), axis=1)
    draft_local = jnp.sum(jnp.exp(draft_logits - draft_max[:, None]), axis=1)
    target_total, draft_total, target_pick, draft_pick = lax.psum(
        (target_local, draft_local, target_sel, draft_sel), ("wide", "narrow")
    )
    target_norm = target_max + jnp.log(target_total)
    draft_norm = draft_max + jnp.log(draft_total)
    target_logprob = target_logits - target_norm[:, None]
    draft_logprob = draft_logits - draft_norm[:, None]
    excess = jnp.maximum(jnp.exp(target_logprob) - jnp.exp(draft_logprob), 0.0)
    leftover = lax.psum(jnp.sum(excess, axis=1), ("wide", "narrow"))
    residual = excess / jnp.maximum(leftover, 0.25)[:, None]
    acceptance = jnp.exp(jnp.minimum(0.0, target_pick - target_norm - (draft_pick - draft_norm)))
    return (target_logprob, draft_logprob, residual, acceptance, leftover)


def solution(mesh):
    placed = (
        P(("wide", "narrow"), None),
        P(None, ("wide", "narrow")),
        P(("wide", "narrow"), None),
        P(None, ("wide", "narrow")),
        P(),
    )
    return jax.shard_map(
        on_device,
        mesh=mesh,
        in_specs=placed,
        out_specs=(
            P(None, ("wide", "narrow")),
            P(None, ("wide", "narrow")),
            P(None, ("wide", "narrow")),
            P(),
            P(),
        ),
        check_vma=False,
    )
```

profile of v0, /device:TPU:0, one launch (start us, length us, event | category | flops | bytes accessed | tf_op | source)
XLA Modules:
  0.0 666.6 jit_solution(9454131717809929759)
XLA Ops:
  7.2 0.0 all-gather.7.cloned.1.call-start
  7.2 0.7 all-gather.7.cloned.1.call-update
  7.9 0.0 all-gather.5.cloned.1.call-start
  7.9 0.7 all-gather.5.cloned.1.call-update
  8.7 201.6 %all-gather.7.cloned.1.call-done = bf16[128,4,4096]{2,1,0:T(4,128)(2,1)} async-done(((bf16[1,4,4096]{2,1,0:T(4,128)(2,1)}), bf16[128,4,4096]{2,1,0:T(4,128)(2,1)}) %all-gather.7.cloned.1.call-update) | async-done | bytes 4194320 | tf_op jit(solution)/shard_map/all_gather | solution.py:16
  210.3 6.9 %reshape.23 = bf16[512,4096]{1,0:T(8,128)(2,1)} reshape(bf16[128,4,4096]{2,1,0:T(4,128)(2,1)} %all-gather.7.cloned.1.call-done) | data formatting | bytes 8388608
  217.2 5.9 fusion.4
  223.1 201.3 %all-gather.5.cloned.1.call-done = bf16[128,4,16384]{2,1,0:T(4,128)(2,1)} async-done(((bf16[1,4,16384]{2,1,0:T(4,128)(2,1)}), bf16[128,4,16384]{2,1,0:T(4,128)(2,1)}) %all-gather.5.cloned.1.call-update) | async-done | bytes 16777232 | tf_op jit(solution)/shard_map/all_gather | solution.py:11
  424.5 23.7 %reshape.21 = bf16[512,16384]{1,0:T(8,128)(2,1)} reshape(bf16[128,4,16384]{2,1,0:T(4,128)(2,1)} %all-gather.5.cloned.1.call-done) | data formatting | bytes 33554432
  448.2 0.0 copy-start.2
  448.2 14.9 %fusion.3 = (f32[512]{0:T(512)S(1)}, f32[512,512]{0,1:T(8,128)S(1)}) fusion(bf16[512,16384]{1,0:T(8,128)(2,1)} %reshape.21, bf16[16384,512]{1,0:T(8,128)(2,1)} %param.6), kind=kOutput, calls=%fused_computation.16 | convolution fusion | flops 8590196736 | bytes 34605056 | tf_op jit(solution)/shard_map/dot_general | solution.py:10
  463.0 0.0 copy-start
  463.0 63.3 %all-reduce.2 = (f32[512]{0:T(512)S(1)}, f32[512]{0:T(512)S(1)}) all-reduce(f32[512]{0:T(512)S(1)} %get-tuple-element.31, f32[512]{0:T(512)S(1)} %get-tuple-element.33), channel_id=1, replica_groups=mesh['wide'=32,'narrow'=4] {'wide','narrow'}, use_global_device_ids=true, to_apply=%region_1.2 | all-reduce | flops 1024 | bytes 8192 | tf_op jit(solution)/shard_map/pmax | solution.py:26
  526.3 0.0 copy-done.2
  526.3 0.5 fusion
  526.8 62.7 %all-reduce.1 = (f32[512]{0:T(512)S(1)}, f32[512]{0:T(512)S(1)}) all-reduce(f32[512]{0:T(512)S(1)} %get-tuple-element.16, f32[512]{0:T(512)S(1)} %get-tuple-element.19), channel_id=1, replica_groups=mesh['wide'=32,'narrow'=4] {'wide','narrow'}, use_global_device_ids=true, to_apply=%region_3.4 | all-reduce | flops 1024 | bytes 8192 | tf_op jit(solution)/shard_map/psum | solution.py:29
  589.5 0.0 copy-done
  589.5 1.6 fusion.2
  591.0 63.9 %all-reduce = (f32[512]{0:T(512)S(1)}, f32[512]{0:T(512)S(1)}, f32[512]{0:T(512)S(1)}) all-reduce(f32[512]{0:T(512)S(1)} %get-tuple-element.28, f32[512]{0:T(512)S(1)} %get-tuple-element.20, f32[512]{0:T(512)S(1)} %get-tuple-element.15), channel_id=1, replica_groups=mesh['wide'=32,'narrow'=4] {'wide','narrow'}, use_global_device_ids=true, to_apply=%region_9.10 | all-reduce | flops 1536 | bytes 12288 | tf_op jit(solution)/shard_map/psum | solution.py:37
  655.0 0.0 copy-start.1
  655.0 1.3 copy.13
  656.3 1.3 copy.14
  657.6 0.3 broadcast_divide_fusion
  657.9 1.3 copy.15
  659.2 0.6 minimum_exponential_fusion
  659.8 0.0 copy-done.1
  (3 shorter events, 0.0 us)
Async XLA Ops:
  7.2 203.1 %all-gather.7.cloned.1.call-start = ((), (), s32[]{:S(2)}) async-start(), calls=%async_computation.1 | async-start | bytes 4227072 | tf_op jit(solution)/shard_map/all_gather | solution.py:16
  7.9 416.6 %all-gather.5.cloned.1.call-start = ((), (), s32[]{:S(2)}) async-start(), calls=%async_computation | async-start | bytes 16908288 | tf_op jit(solution)/shard_map/all_gather | solution.py:11
  448.2 78.2 %copy-start.2 = (s32[512]{0:T(512)S(1)}, s32[512]{0:T(512)}, u32[]{:S(2)}) copy-start(s32[512]{0:T(512)} %param.9) | copy-start | bytes 6148
  463.0 126.4 %copy-start = (f32[512,512]{0,1:T(8,128)}, f32[512,512]{0,1:T(8,128)S(1)}, u32[]{:S(2)}) copy-start(f32[512,512]{0,1:T(8,128)S(1)} %get-tuple-element.32) | copy-start | bytes 3145732
  655.0 4.8 copy-start.1
Sparse Core Ops, SparseCore 0:
  9.7 200.5 all-gather.6
  212.0 212.4 all-gather.4
where the time goes:
time: 668 us; the launch traced here: 667 us
  waiting for transfers between devices  404 us (60%)
  blocking collectives  190 us (28%)
  local copies, waits for them, and re-layouts  34.5 us (5%)
  matrix products  20.8 us (3%)
  between operations  14.1 us (2%)
    all_gather x1, waiting for transfers between devices, on_device(): lax.all_gather(draft_hidden, ('wide', 'narrow'), axis=0, tiled=True)  202 us
    all_gather x1, waiting for transfers between devices, on_device(): lax.all_gather(target_hidden, ('wide', 'narrow'), axis=0, tiled=True)  201 us
    psum x1, blocking collectives, on_device(): leftover = lax.psum(jnp.sum(excess, axis=1), ('wide', 'narrow'))  63.9 us
    pmax x1, blocking collectives, on_device(): lax.pmax((target_top, draft_top), ('wide', 'narrow'))  63.3 us
    psum x1, blocking collectives, on_device(): lax.psum((target_local, draft_local, target_sel, draft_sel), ('wide', 'na...  62.7 us
    unnamed x11, local copies, waits for them, and re-layouts  34.5 us
    dot_general x1, matrix products, on_device(): jnp.dot(lax.all_gather(target_hidden, ('wide', 'narrow'), axis=0, tiled=T...  14.9 us
  transfers between devices with their start and end apart: 2, of which 2 were waited for; matrix products, arithmetic and copies ran while one was open for 2% of the time, Pallas kernels for 0%

commit v1 on v0

v1 whole, which is shorter than its diff:
```python
import functools

import jax
import jax.numpy as jnp
from jax import lax
from jax.experimental import pallas as pl
from jax.experimental.pallas import tpu as pltpu
from jax.sharding import PartitionSpec as P

MESH = pl.DeviceIdType.MESH
T = 128
ORDERS = (("x", "y", "z"), ("y", "z", "x"), ("z", "x", "y"))
SPLIT = (("d", (3, 3, 2)), ("t", (4, 4, 5)), ("t", (4, 4, 4)), ("t", (2, 2, 3)))


def make_units():
    units, used = [], {"d": 0, "t": 0}
    for kind, sizes in SPLIT:
        for order, size in enumerate(sizes):
            units.append((order, kind, used[kind] * T, size * T))
            used[kind] += size
    return units


UNITS = make_units()
GROUPS = len(SPLIT)


def view(sel):
    whole = slice(None)
    x = sel["x"]
    if x == "all":
        hi, lo = whole, whole
    elif isinstance(x, tuple):
        hi, lo = x[1], whole
    else:
        hi, lo = lax.div(x, 2), lax.rem(x, 2)
    rest = []
    for name in ("y", "z"):
        v = sel[name]
        if isinstance(v, str):
            rest.append(whole)
        elif isinstance(v, tuple):
            rest.append(pl.ds(2 * v[1], 2))
        else:
            rest.append(v)
    return (hi, rest[0], rest[1], lo)


def kernel(ht_ref, wt_ref, hd_ref, wd_ref, tok_ref, lt_ref, ld_ref, stat_ref, *scratch):
    n_units = len(UNITS)
    hb = scratch[:n_units]
    wb = scratch[n_units : 2 * n_units]
    (stage_t, stage_d, acc_t, acc_d, part_t, part_d, tok_f, near, far,
     gs, gr, wl, ws, wr, es, er, el, ps, pr, ns, nr, fs, fr, osem) = scratch[2 * n_units :]
    w, n = lax.axis_index("wide"), lax.axis_index("narrow")
    pos = {"x": lax.div(n, 2) * 2 + lax.rem(w, 2), "y": lax.div(w, 8), "z": lax.rem(lax.div(w, 2), 4)}
    c = lax.rem(n, 2)

    def device(dx=0, dy=0, dz=0, dc=0):
        x = lax.rem(pos["x"] + dx, 4)
        y = lax.rem(pos["y"] + dy, 4)
        z = lax.rem(pos["z"] + dz, 4)
        return ((y * 4 + z) * 2 + lax.rem(x, 2), lax.div(x, 2) * 2 + lax.rem(c + dc, 2))

    def shift(dim, by):
        return device(**{"d" + dim: by})

    def remote(src, dst, send, recv, to):
        return pltpu.make_async_remote_copy(
            src_ref=src, dst_ref=dst, send_sem=send, recv_sem=recv, device_id=to, device_id_type=MESH
        )

    partner = device(dc=1)

    local = []
    for u, (order, kind, start, size) in enumerate(UNITS):
        ref = wt_ref if kind == "t" else wd_ref
        local.append(pltpu.make_async_copy(ref.at[c, :, pl.ds(start, size), :], wb[u].at[0], wl.at[u]))
        local[-1].start()
    own_t = pltpu.make_async_copy(
        ht_ref.at[:, pl.ds(pl.multiple_of(c * 8192 + lax.div(n, 2) * 4096, T), 4096)], stage_t.at[n], el.at[0])
    own_d = pltpu.make_async_copy(
        hd_ref.at[:, pl.ds(pl.multiple_of(c * 2048 + lax.div(n, 2) * 1024, T), 1024)], stage_d.at[n], el.at[1])
    own_t.start()
    own_d.start()

    near_offs = [(a, b) for a in range(4) for b in range(2) if (a, b) != (0, 0)]
    far_offs = [(a, b) for a in range(4) for b in range(4) if (a, b) != (0, 0)]
    barrier = pltpu.get_barrier_semaphore()
    for a, b in near_offs:
        pl.semaphore_signal(barrier, inc=1, device_id=device(dx=a, dc=b), device_id_type=MESH)
    for a, b in far_offs:
        pl.semaphore_signal(barrier, inc=1, device_id=device(dy=a, dz=b), device_id_type=MESH)
    pl.semaphore_wait(barrier, len(near_offs) + len(far_offs))

    swaps = []
    for j in range(1, 4):
        to = lax.rem(n + j, 4)
        frm = lax.rem(n + 4 - j, 4)
        qt = pl.multiple_of(lax.rem(to, 2) * 8192 + lax.div(to, 2) * 4096, T)
        qd = pl.multiple_of(lax.rem(to, 2) * 2048 + lax.div(to, 2) * 1024, T)
        send_d = remote(hd_ref.at[:, pl.ds(qd, 1024)], stage_d.at[n], es.at[1, j], er.at[1, j], (w, to))
        send_t = remote(ht_ref.at[:, pl.ds(qt, 4096)], stage_t.at[n], es.at[0, j], er.at[0, j], (w, to))
        send_d.start()
        send_t.start()
        swaps.append(send_d)
        swaps.append(send_t)
    lent = []
    for u, (order, kind, start, size) in enumerate(UNITS):
        ref = wt_ref if kind == "t" else wd_ref
        lent.append(remote(ref.at[1 - c, :, pl.ds(start, size), :], wb[u].at[1], ws.at[u], wr.at[u], partner))
        lent[-1].start()
    own_t.wait()
    own_d.wait()
    for s in swaps:
        s.wait_recv()

    sends = []

    def send(u, k, src, to):
        copy = remote(src, src, gs.at[u, k], gr.at[u, k], to)
        copy.start()
        sends.append(copy)
        return copy

    arriving = {}
    xh, xl = lax.div(pos["x"], 2), lax.rem(pos["x"], 2)

    def line(order, c2, part="all"):
        d1, d2, d3 = order
        return view({d1: part, d2: c2, d3: pos[d3]})

    def plane(order, c3, part="all"):
        d1, d2, d3 = order
        return view({d1: "all", d2: part, d3: c3})

    def up(dim):
        return lax.rem(pos[dim] + 1, 4)

    def down(dim):
        return lax.rem(pos[dim] + 3, 4)

    def phase1(u):
        o, kind, start, size = UNITS[u]
        order = ORDERS[o]
        stage = stage_t if kind == "t" else stage_d
        rows = [stage[j, :, start : start + size].astype(jnp.float32) for j in range(4)]
        hb[u][xh, pos["y"], pos["z"], xl] = jnp.concatenate(rows, axis=0).astype(jnp.bfloat16)
        mine = hb[u].at[xh, pos["y"], pos["z"], xl]
        arriving[u, 1] = [send(u, k, mine, shift(order[0], by)) for k, by in ((0, 1), (1, 3), (2, 2))]

    def arrived(u, phase):
        for copy in arriving[u, phase]:
            copy.wait_recv()

    def phase2a(u):
        order = ORDERS[UNITS[u][0]]
        arrived(u, 1)
        mine = hb[u].at[line(order, pos[order[1]])]
        arriving[u, 2] = [send(u, k, mine, shift(order[1], by)) for k, by in ((3, 1), (4, 3))]

    def phase2b(u):
        order = ORDERS[UNITS[u][0]]
        arrived(u, 2)
        d = order[1]
        arriving[u, 3] = [
            send(u, 5, hb[u].at[line(order, down(d), ("half", 0))], shift(d, 1)),
            send(u, 6, hb[u].at[line(order, up(d), ("half", 1))], shift(d, 3)),
        ]

    def phase3a(u):
        order = ORDERS[UNITS[u][0]]
        arrived(u, 3)
        mine = hb[u].at[plane(order, pos[order[2]])]
        arriving[u, 4] = [send(u, k, mine, shift(order[2], by)) for k, by in ((7, 1), (8, 3))]

    def phase3b(u):
        order = ORDERS[UNITS[u][0]]
        arrived(u, 4)
        d = order[2]
        arriving[u, 5] = [
            send(u, 9, hb[u].at[plane(order, down(d), ("half", 0))], shift(d, 1)),
            send(u, 10, hb[u].at[plane(order, up(d), ("half", 1))], shift(d, 3)),
        ]

    begun = set()

    def multiply(u):
        o, kind, start, size = UNITS[u]
        arrived(u, 5)
        local[u].wait()
        lent[u].wait_recv()
        acc = acc_t if kind == "t" else acc_d
        first = kind not in begun
        begun.add(kind)

        def body(i, carry):
            side, col = lax.div(i, 2), pl.multiple_of(lax.rem(i, 2) * 256, 256)
            lhs = jnp.concatenate([hb[u][0].reshape(512, size), hb[u][1].reshape(512, size)], axis=1)
            rhs = wb[u][side, :, :, pl.ds(col, 256)].reshape(2 * size, 256)
            res = jnp.dot(lhs, rhs, preferred_element_type=jnp.float32)
            if first:
                acc[side, :, pl.ds(col, 256)] = res
            else:
                acc[side, :, pl.ds(col, 256)] += res
            return carry

        lax.fori_loop(0, 4, body, 0)

    def every(f, g):
        for u in range(3 * g, 3 * g + 3):
            f(u)

    def give(k, acc, part):
        copy = remote(acc.at[1], part, ps.at[k], pr.at[k], partner)
        copy.start()
        sends.append(copy)
        return copy

    def columns(row):
        return jnp.broadcast_to(row, (128, 128)).T

    def totals(acc, part, base):
        def body(j, carry):
            rows = pl.ds(pl.multiple_of(j * 128, 128), 128)
            logits = acc[0, rows, :] + part[rows, :]
            acc[0, rows, :] = logits
            tiles = [logits[:, 128 * t : 128 * t + 128] for t in range(4)]
            most = jnp.maximum(jnp.maximum(tiles[0], tiles[1]), jnp.maximum(tiles[2], tiles[3]))
            top = jnp.max(most.T, axis=0, keepdims=True)
            top_col = columns(top)
            e = [jnp.exp(t - top_col) for t in tiles]
            total = jnp.sum(((e[0] + e[1]) + (e[2] + e[3])).T, axis=0, keepdims=True)
            near[0, 8, pl.ds(base + j, 1), :] = top + jnp.log(total)
            return carry

        lax.fori_loop(0, 4, body, 0)

    near_me = pos["x"] * 2 + c
    far_me = pos["y"] * 4 + pos["z"]

    def spread(buf, ss, rs, r, me, count, value, targets):
        buf[r, me] = value
        copies = [remote(buf.at[r, me], buf.at[r, me], ss.at[r, i], rs.at[r], to) for i, to in enumerate(targets)]
        for copy in copies:
            copy.start()
        sends.extend(copies)
        full = buf.at[r, pl.ds(0, count - 1)]
        remote(full, full, ss.at[r, 0], rs.at[r], targets[0]).wait_recv()
        return buf[r, 0:count]

    near_to = [device(dx=a, dc=b) for a, b in near_offs]
    far_to = [device(dy=a, dz=b) for a, b in far_offs]

    def merge(values):
        top = jnp.max(values, axis=0)
        return top + jnp.log(jnp.sum(jnp.exp(values - top[None]), axis=0))

    for g in range(GROUPS):
        every(phase1, g)
    every(phase2a, 0)
    every(phase2a, 1)
    every(phase2b, 0)
    every(phase2a, 2)
    every(phase2a, 3)
    every(phase3a, 0)
    every(phase2b, 1)
    every(phase3a, 1)
    every(phase2b, 2)
    every(phase2b, 3)
    every(phase3b, 0)
    every(phase3a, 2)
    every(phase3b, 1)
    every(phase3a, 3)
    every(multiply, 0)
    gave_d = give(0, acc_d, part_d)
    every(phase3b, 2)
    every(multiply, 1)
    every(phase3b, 3)
    gave_d.wait_recv()
    totals(acc_d, part_d, 4)
    every(multiply, 2)
    every(multiply, 3)
    gave_t = give(1, acc_t, part_t)
    gave_t.wait_recv()
    totals(acc_t, part_t, 0)

    lse = merge(spread(near, ns, nr, 0, near_me, 8, near[0, 8], near_to))
    lse = merge(spread(far, fs, fr, 0, far_me, 16, lse, far_to))
    near[0, 8] = lse
    stat_ref[0:8, :] = lse

    out_t = pltpu.make_async_copy(acc_t.at[0], lt_ref, osem.at[0])
    out_d = pltpu.make_async_copy(acc_d.at[0], ld_ref, osem.at[1])
    out_t.start()
    out_d.start()

    offset = (w * 4 + n) * 512
    tok_f[...] = (tok_ref[...] - offset).astype(jnp.float32)

    def mass(j, carry):
        rows = pl.ds(pl.multiple_of(j * 128, 128), 128)
        lt, ld = acc_t[0, rows, :], acc_d[0, rows, :]
        t_col = columns(near[0, 8, pl.ds(j, 1), :])
        d_col = columns(near[0, 8, pl.ds(4 + j, 1), :])
        tok = columns(tok_f[pl.ds(j, 1), :])
        lanes = lax.broadcasted_iota(jnp.int32, (128, 128), 1).astype(jnp.float32)
        kept, picked = None, None
        for t in range(4):
            lp = lt[:, 128 * t : 128 * t + 128] - t_col
            dp = ld[:, 128 * t : 128 * t + 128] - d_col
            e = jnp.maximum(jnp.exp(lp) - jnp.exp(dp), 0.0)
            p = jnp.where(tok == lanes + 128.0 * t, lp - dp, 0.0)
            kept = e if kept is None else kept + e
            picked = p if picked is None else picked + p
        near[1, 8, pl.ds(j, 1), :] = jnp.sum(kept.T, axis=0, keepdims=True)
        near[1, 8, pl.ds(4 + j, 1), :] = jnp.sum(picked.T, axis=0, keepdims=True)
        return carry

    lax.fori_loop(0, 4, mass, 0)
    both = jnp.sum(spread(near, ns, nr, 1, near_me, 8, near[1, 8], near_to), axis=0)
    both = jnp.sum(spread(far, fs, fr, 1, far_me, 16, both, far_to), axis=0)
    stat_ref[8:12, :] = both[0:4]
    stat_ref[12:16, :] = jnp.exp(jnp.minimum(both[4:8], 0.0))

    out_t.wait()
    out_d.wait()
    for s in swaps + lent + sends:
        s.wait_send()


def on_device(target_hidden, target_weight, draft_hidden, draft_weight, draft_tokens):
    vmem, anywhere = pl.BlockSpec(memory_space=pltpu.VMEM), pl.BlockSpec(memory_space=pl.ANY)
    n_units = len(UNITS)
    dma = pltpu.SemaphoreType.DMA
    f32 = jnp.float32
    lt, ld, stat = pl.pallas_call(
        kernel,
        name="verify",
        out_shape=(
            jax.ShapeDtypeStruct((512, 512), f32),
            jax.ShapeDtypeStruct((512, 512), f32),
            jax.ShapeDtypeStruct((16, 128), f32),
        ),
        in_specs=[anywhere, anywhere, anywhere, anywhere, vmem],
        out_specs=(anywhere, anywhere, vmem),
        scratch_shapes=(
            [pltpu.VMEM((2, 4, 4, 2, 16, size), jnp.bfloat16) for _, _, _, size in UNITS]
            + [pltpu.VMEM((2, 2, size, 512), jnp.bfloat16) for _, _, _, size in UNITS]
            + [
                pltpu.VMEM((4, 4, 4096), jnp.bfloat16),
                pltpu.VMEM((4, 4, 1024), jnp.bfloat16),
                pltpu.VMEM((2, 512, 512), f32),
                pltpu.VMEM((2, 512, 512), f32),
                pltpu.VMEM((512, 512), f32),
                pltpu.VMEM((512, 512), f32),
                pltpu.VMEM((4, 128), f32),
                pltpu.VMEM((2, 9, 8, 128), f32),
                pltpu.VMEM((2, 16, 8, 128), f32),
                dma((n_units, 11)), dma((n_units, 11)),
                dma((n_units,)), dma((n_units,)), dma((n_units,)),
                dma((2, 4)), dma((2, 4)), dma((2,)),
                dma((2,)), dma((2,)),
                dma((2, 7)), dma((2,)),
                dma((2, 15)), dma((2,)),
                dma((2,)),
            ]
        ),
        compiler_params=pltpu.CompilerParams(
            collective_id=0, has_side_effects=True, vmem_limit_bytes=56 * 2**20
        ),
    )(
        target_hidden,
        target_weight.reshape(2, 2, 4096, 512),
        draft_hidden,
        draft_weight.reshape(2, 2, 1024, 512),
        draft_tokens.reshape(4, 128),
    )
    t_norm = stat[0:4].reshape(512, 1)
    d_norm = stat[4:8].reshape(512, 1)
    leftover = stat[8:12].reshape(512)
    t_log, d_log = lt - t_norm, ld - d_norm
    excess = jnp.maximum(jnp.exp(t_log) - jnp.exp(d_log), 0.0)
    residual = excess / jnp.maximum(leftover, 0.25)[:, None]
    return t_log, d_log, residual, stat[12:16].reshape(512), leftover


def solution(mesh):
    placed = (
        P(("wide", "narrow"), None),
        P(None, ("wide", "narrow")),
        P(("wide", "narrow"), None),
        P(None, ("wide", "narrow")),
        P(),
    )
    return jax.shard_map(
        on_device,
        mesh=mesh,
        in_specs=placed,
        out_specs=(
            P(None, ("wide", "narrow")),
            P(None, ("wide", "narrow")),
            P(None, ("wide", "narrow")),
            P(),
            P(),
        ),
        check_vma=False,
    )
```

time: 668 us -> 99.1 us (0.15)
  waiting for transfers between devices: 404 us -> 0 us
  blocking collectives: 190 us -> 0 us
  Pallas kernels: 0 us -> 91.8 us
  local copies, waits for them, and re-layouts: 34.5 us -> 1.34 us
  matrix products: 20.8 us -> 0 us
  between operations: 14.1 us -> 0.64 us
    all_gather x2 -> x0, waiting for transfers between devices: 403 us -> none  [the longest x1 202 us: on_device(): lax.all_gather(draft_hidden, ('wide', 'narrow'), axis=0, tiled=True)]
    psum x2 -> x0, blocking collectives: 127 us -> none  [the longest x1 63.9 us: on_device(): leftover = lax.psum(jnp.sum(excess, axis=1), ('wide', 'narrow'))]
    pallas_call x0 -> x1, Pallas kernels: none -> 91.8 us  [on_device(): pl.pallas_call(kernel, name='verify', out_shape=(jax.ShapeDtypeStruct((51...]
    pmax x1 -> x0, blocking collectives: 63.3 us -> none  [on_device(): lax.pmax((target_top, draft_top), ('wide', 'narrow'))]
    unnamed x11 -> x0, local copies, waits for them, and re-layouts: 34.5 us -> none
    dot_general x2 -> x0, matrix products: 20.8 us -> none  [the longest x1 14.9 us: on_device(): jnp.dot(lax.all_gather(target_hidden, ('wide', 'narrow'), axis=0, tiled=T...]
  transfers between devices with their start and end apart: 2 -> 0, of which waited for: 2 -> 0; matrix products, arithmetic and copies ran while one was open for 2% -> 0% of each run, Pallas kernels for 0% -> 0%
where the time goes in v1:
time: 99.1 us; the launch traced here: 98.6 us
  Pallas kernels  91.8 us (93%)
  other arithmetic  4.82 us (5%)
  local copies, waits for them, and re-layouts  1.34 us (1%)
    pallas_call x1, Pallas kernels, on_device(): pl.pallas_call(kernel, name='verify', out_shape=(jax.ShapeDtypeStruct((51...  91.8 us
    div x1, other arithmetic, on_device(): residual = excess / jnp.maximum(leftover, 0.25)[:, None]  3.56 us

profile of v1, /device:TPU:0, one launch (start us, length us, event | category | flops | bytes accessed | tf_op | source)
XLA Modules:
  0.0 98.6 jit_solution(11602267489705976461)
XLA Ops:
  0.6 91.8 %verify.1 = (f32[512,512]{1,0:T(8,128)}, f32[512,512]{1,0:T(8,128)}, f32[16,128]{1,0:T(8,128)}) custom-call(bf16[4,16384]{1,0:T(4,128)(2,1)} %ht_ref.1, bf16[2,2,4096,512]{3,2,1,0:T(8,128)(2,1)} %bitcast.12, bf16[4,4096]{1,0:T(4,128)(2,1)} %hd_ref.1, bf16[2,2,1024,512]{3,2,1,0:T(8,128)(2,1)} %bitcast.13, s32[4,128]{1,0:T(4,128)} %bitcast.14), custom_call_target="tpu_custom_call" | custom-call | tf_op jit(solution)/shard_map/verify/pallas_call | solution.py:338
  92.4 1.3 %broadcast_maximum_fusion = (f32[512]{0:T(512)S(1)}, f32[512]{0:T(512)}) fusion(f32[16,128]{1,0:T(8,128)} %get-tuple-element.9), kind=kLoop, calls=%fused_computation.7 | loop fusion | flops 512 | bytes 6144 | tf_op jit(solution)/shard_map/max | solution.py:385
  93.7 1.3 %slice_bitcast_fusion = (f32[512]{0:T(512)}, f32[512]{0:T(512)S(1)}, f32[512]{0:T(512)S(1)}) fusion(f32[16,128]{1,0:T(8,128)} %get-tuple-element.9), kind=kLoop, calls=%fused_computation.3 | loop fusion | bytes 12288 | tf_op jit(solution)/shard_map/reshape | solution.py:386
  95.0 3.6 %maximum_divide_fusion = (f32[512,512]{1,0:T(8,128)}, f32[512,512]{1,0:T(8,128)}, f32[512,512]{1,0:T(8,128)}) fusion(f32[512]{0:T(512)S(1)} %get-tuple-element.14, f32[512,512]{1,0:T(8,128)} %get-tuple-element.10, f32[512]{0:T(512)S(1)} %get-tuple-element.17, f32[512,512]{1,0:T(8,128)} %get-tuple-element.8, f32[512]{0:T(512)S(1)} %get-tuple-element.18), kind=kLoop, calls=%fused_computation | loop fusion | flops 1310720 | bytes 5249024 | tf_op jit(solution)/shard_map/div | solution.py:385

commit v2 on v1

--- a/solution.py
+++ b/solution.py
@@ -10,7 +10,7 @@
 MESH = pl.DeviceIdType.MESH
 T = 128
 ORDERS = (("x", "y", "z"), ("y", "z", "x"), ("z", "x", "y"))
-SPLIT = (("d", (3, 3, 2)), ("t", (4, 4, 5)), ("t", (4, 4, 4)), ("t", (2, 2, 3)))
+SPLIT = (("d", (3, 3, 2)), ("t", (4, 4, 4)), ("t", (3, 3, 4)), ("t", (2, 2, 2)), ("t", (1, 1, 2)))
 
 
 def make_units():
@@ -32,7 +32,7 @@
     if x == "all":
         hi, lo = whole, whole
     elif isinstance(x, tuple):
-        hi, lo = x[1], whole
+        hi, lo = whole, x[1]
     else:
         hi, lo = lax.div(x, 2), lax.rem(x, 2)
     rest = []
@@ -44,15 +44,15 @@
             rest.append(pl.ds(2 * v[1], 2))
         else:
             rest.append(v)
-    return (hi, rest[0], rest[1], lo)
-
-
-def kernel(ht_ref, wt_ref, hd_ref, wd_ref, tok_ref, lt_ref, ld_ref, stat_ref, *scratch):
+    return (lo, rest[0], rest[1], hi)
+
+
+def kernel(ht_ref, wt_ref, hd_ref, wd_ref, tok_ref, lt_ref, ld_ref, ex_ref, stat_ref, *scratch):
     n_units = len(UNITS)
     hb = scratch[:n_units]
     wb = scratch[n_units : 2 * n_units]
-    (stage_t, stage_d, acc_t, acc_d, part_t, part_d, tok_f, near, far,
-     gs, gr, wl, ws, wr, es, er, el, ps, pr, ns, nr, fs, fr, osem) = scratch[2 * n_units :]
+    (stage_t, stage_d, acc_t, acc_d, part_t, part_d, tok_i, tok_f, near, far,
+     gs, gr, wl, ws, wr, es, er, el, ps, pr, ns, nr, fs, fr) = scratch[2 * n_units :]
     w, n = lax.axis_index("wide"), lax.axis_index("narrow")
     pos = {"x": lax.div(n, 2) * 2 + lax.rem(w, 2), "y": lax.div(w, 8), "z": lax.rem(lax.div(w, 2), 4)}
     c = lax.rem(n, 2)
@@ -72,6 +72,8 @@
         )
 
     partner = device(dc=1)
+    xh, xl = lax.div(pos["x"], 2), lax.rem(pos["x"], 2)
+    me = xl * 2 + c
 
     local = []
     for u, (order, kind, start, size) in enumerate(UNITS):
@@ -79,14 +81,17 @@
         local.append(pltpu.make_async_copy(ref.at[c, :, pl.ds(start, size), :], wb[u].at[0], wl.at[u]))
         local[-1].start()
     own_t = pltpu.make_async_copy(
-        ht_ref.at[:, pl.ds(pl.multiple_of(c * 8192 + lax.div(n, 2) * 4096, T), 4096)], stage_t.at[n], el.at[0])
+        ht_ref.at[:, pl.ds(pl.multiple_of(c * 8192 + xl * 4096, T), 4096)], stage_t.at[me], el.at[0])
     own_d = pltpu.make_async_copy(
-        hd_ref.at[:, pl.ds(pl.multiple_of(c * 2048 + lax.div(n, 2) * 1024, T), 1024)], stage_d.at[n], el.at[1])
+        hd_ref.at[:, pl.ds(pl.multiple_of(c * 2048 + xl * 1024, T), 1024)], stage_d.at[me], el.at[1])
+    own_tok = pltpu.make_async_copy(tok_ref, tok_i, el.at[2])
     own_t.start()
     own_d.start()
-
-    near_offs = [(a, b) for a in range(4) for b in range(2) if (a, b) != (0, 0)]
-    far_offs = [(a, b) for a in range(4) for b in range(4) if (a, b) != (0, 0)]
+    own_tok.start()
+
+    steps = (0, 1, 2, 1)
+    near_offs = sorted(((a, b) for a in range(4) for b in range(2) if (a, b) != (0, 0)), key=lambda o: -2 * steps[o[0]] - o[1])
+    far_offs = sorted(((a, b) for a in range(4) for b in range(4) if (a, b) != (0, 0)), key=lambda o: -steps[o[0]] - steps[o[1]])
     barrier = pltpu.get_barrier_semaphore()
     for a, b in near_offs:
         pl.semaphore_signal(barrier, inc=1, device_id=device(dx=a, dc=b), device_id_type=MESH)
@@ -96,16 +101,15 @@
 
     swaps = []
     for j in range(1, 4):
-        to = lax.rem(n + j, 4)
-        frm = lax.rem(n + 4 - j, 4)
-        qt = pl.multiple_of(lax.rem(to, 2) * 8192 + lax.div(to, 2) * 4096, T)
-        qd = pl.multiple_of(lax.rem(to, 2) * 2048 + lax.div(to, 2) * 1024, T)
-        send_d = remote(hd_ref.at[:, pl.ds(qd, 1024)], stage_d.at[n], es.at[1, j], er.at[1, j], (w, to))
-        send_t = remote(ht_ref.at[:, pl.ds(qt, 4096)], stage_t.at[n], es.at[0, j], er.at[0, j], (w, to))
-        send_d.start()
-        send_t.start()
-        swaps.append(send_d)
-        swaps.append(send_t)
+        to = lax.rem(me + j, 4)
+        to_c, to_l = lax.rem(to, 2), lax.div(to, 2)
+        target = ((pos["y"] * 4 + pos["z"]) * 2 + to_l, xh * 2 + to_c)
+        qt = pl.multiple_of(to_c * 8192 + to_l * 4096, T)
+        qd = pl.multiple_of(to_c * 2048 + to_l * 1024, T)
+        swaps.append(remote(hd_ref.at[:, pl.ds(qd, 1024)], stage_d.at[me], es.at[1, j], er.at[1, j], target))
+        swaps.append(remote(ht_ref.at[:, pl.ds(qt, 4096)], stage_t.at[me], es.at[0, j], er.at[0, j], target))
+    for s in swaps:
+        s.start()
     lent = []
     for u, (order, kind, start, size) in enumerate(UNITS):
         ref = wt_ref if kind == "t" else wd_ref
@@ -125,7 +129,6 @@
         return copy
 
     arriving = {}
-    xh, xl = lax.div(pos["x"], 2), lax.rem(pos["x"], 2)
 
     def line(order, c2, part="all"):
         d1, d2, d3 = order
@@ -146,8 +149,8 @@
         order = ORDERS[o]
         stage = stage_t if kind == "t" else stage_d
         rows = [stage[j, :, start : start + size].astype(jnp.float32) for j in range(4)]
-        hb[u][xh, pos["y"], pos["z"], xl] = jnp.concatenate(rows, axis=0).astype(jnp.bfloat16)
-        mine = hb[u].at[xh, pos["y"], pos["z"], xl]
+        hb[u][xl, pos["y"], pos["z"], xh] = jnp.concatenate(rows, axis=0).astype(jnp.bfloat16)
+        mine = hb[u].at[xl, pos["y"], pos["z"], xh]
         arriving[u, 1] = [send(u, k, mine, shift(order[0], by)) for k, by in ((0, 1), (1, 3), (2, 2))]
 
     def arrived(u, phase):
@@ -186,45 +189,48 @@
 
     begun = set()
 
-    def multiply(u):
+    def multiply(u, sides=(1, 0), again=False):
         o, kind, start, size = UNITS[u]
-        arrived(u, 5)
-        local[u].wait()
-        lent[u].wait_recv()
+        if not again:
+            arrived(u, 5)
+            local[u].wait()
+            lent[u].wait_recv()
         acc = acc_t if kind == "t" else acc_d
         first = kind not in begun
         begun.add(kind)
-
-        def body(i, carry):
-            side, col = lax.div(i, 2), pl.multiple_of(lax.rem(i, 2) * 256, 256)
-            lhs = jnp.concatenate([hb[u][0].reshape(512, size), hb[u][1].reshape(512, size)], axis=1)
-            rhs = wb[u][side, :, :, pl.ds(col, 256)].reshape(2 * size, 256)
-            res = jnp.dot(lhs, rhs, preferred_element_type=jnp.float32)
-            if first:
-                acc[side, :, pl.ds(col, 256)] = res
-            else:
-                acc[side, :, pl.ds(col, 256)] += res
-            return carry
-
-        lax.fori_loop(0, 4, body, 0)
+        lhs = jnp.concatenate([hb[u][0].reshape(512, size), hb[u][1].reshape(512, size)], axis=1)
+        for side in sides:
+            for col in (0, 256):
+                rhs = wb[u][side, :, :, col : col + 256].reshape(2 * size, 256)
+                res = jnp.dot(lhs, rhs, preferred_element_type=jnp.float32)
+                if first:
+                    acc[side, :, col : col + 256] = res
+                else:
+                    acc[side, :, col : col + 256] += res
 
     def every(f, g):
         for u in range(3 * g, 3 * g + 3):
             f(u)
 
+    def given(k, acc, part, j):
+        rows = pl.ds(pl.multiple_of(j * 128, 128), 128)
+        return remote(acc.at[1, rows, :], part.at[rows, :], ps.at[k, j], pr.at[k, j], partner)
+
     def give(k, acc, part):
-        copy = remote(acc.at[1], part, ps.at[k], pr.at[k], partner)
-        copy.start()
-        sends.append(copy)
-        return copy
+        for j in range(4):
+            sends.append(given(k, acc, part, j))
+            sends[-1].start()
 
     def columns(row):
         return jnp.broadcast_to(row, (128, 128)).T
 
-    def totals(acc, part, base):
+    def totals(k, acc, part, base):
         def body(j, carry):
             rows = pl.ds(pl.multiple_of(j * 128, 128), 128)
-            logits = acc[0, rows, :] + part[rows, :]
+            given(k, acc, part, j).wait_recv()
+            mixed = acc[0, rows, :] + part[rows, :]
+            order = [32 * q + r for q in range(4) for r in (0, 16, 8, 24)]
+            logits = jnp.concatenate([mixed[r : r + 8] for r in order], axis=0)
             acc[0, rows, :] = logits
             tiles = [logits[:, 128 * t : 128 * t + 128] for t in range(4)]
             most = jnp.maximum(jnp.maximum(tiles[0], tiles[1]), jnp.maximum(tiles[2], tiles[3]))
@@ -257,47 +263,37 @@
         top = jnp.max(values, axis=0)
         return top + jnp.log(jnp.sum(jnp.exp(values - top[None]), axis=0))
 
-    for g in range(GROUPS):
-        every(phase1, g)
-    every(phase2a, 0)
-    every(phase2a, 1)
-    every(phase2b, 0)
-    every(phase2a, 2)
-    every(phase2a, 3)
+    for phase in (phase1, phase2a, phase2b):
+        for g in range(GROUPS):
+            every(phase, g)
     every(phase3a, 0)
-    every(phase2b, 1)
     every(phase3a, 1)
-    every(phase2b, 2)
-    every(phase2b, 3)
     every(phase3b, 0)
     every(phase3a, 2)
     every(phase3b, 1)
     every(phase3a, 3)
     every(multiply, 0)
-    gave_d = give(0, acc_d, part_d)
+    give(0, acc_d, part_d)
     every(phase3b, 2)
+    every(phase3a, 4)
     every(multiply, 1)
     every(phase3b, 3)
-    gave_d.wait_recv()
-    totals(acc_d, part_d, 4)
+    totals(0, acc_d, part_d, 4)
+    every(phase3b, 4)
     every(multiply, 2)
     every(multiply, 3)
-    gave_t = give(1, acc_t, part_t)
-    gave_t.wait_recv()
-    totals(acc_t, part_t, 0)
+    every(lambda u: multiply(u, (1,)), 4)
+    give(1, acc_t, part_t)
+    every(lambda u: multiply(u, (0,), True), 4)
+    totals(1, acc_t, part_t, 0)
 
     lse = merge(spread(near, ns, nr, 0, near_me, 8, near[0, 8], near_to))
     lse = merge(spread(far, fs, fr, 0, far_me, 16, lse, far_to))
     near[0, 8] = lse
-    stat_ref[0:8, :] = lse
-
-    out_t = pltpu.make_async_copy(acc_t.at[0], lt_ref, osem.at[0])
-    out_d = pltpu.make_async_copy(acc_d.at[0], ld_ref, osem.at[1])
-    out_t.start()
-    out_d.start()
-
+
+    own_tok.wait()
     offset = (w * 4 + n) * 512
-    tok_f[...] = (tok_ref[...] - offset).astype(jnp.float32)
+    tok_f[...] = (tok_i[...] - offset).astype(jnp.float32)
 
     def mass(j, carry):
         rows = pl.ds(pl.multiple_of(j * 128, 128), 128)
@@ -310,7 +306,10 @@
         for t in range(4):
             lp = lt[:, 128 * t : 128 * t + 128] - t_col
             dp = ld[:, 128 * t : 128 * t + 128] - d_col
+            lt_ref[rows, 128 * t : 128 * t + 128] = lp
+            ld_ref[rows, 128 * t : 128 * t + 128] = dp
             e = jnp.maximum(jnp.exp(lp) - jnp.exp(dp), 0.0)
+            ex_ref[rows, 128 * t : 128 * t + 128] = e
             p = jnp.where(tok == lanes + 128.0 * t, lp - dp, 0.0)
             kept = e if kept is None else kept + e
             picked = p if picked is None else picked + p
@@ -321,13 +320,30 @@
     lax.fori_loop(0, 4, mass, 0)
     both = jnp.sum(spread(near, ns, nr, 1, near_me, 8, near[1, 8], near_to), axis=0)
     both = jnp.sum(spread(far, fs, fr, 1, far_me, 16, both, far_to), axis=0)
-    stat_ref[8:12, :] = both[0:4]
-    stat_ref[12:16, :] = jnp.exp(jnp.minimum(both[4:8], 0.0))
-
-    out_t.wait()
-    out_d.wait()
+    stat_ref[...] = both
+
     for s in swaps + lent + sends:
         s.wait_send()
+
+
+def finish(lt_ref, ld_ref, ex_ref, stat_ref, t_ref, d_ref, r_ref, accept_ref, left_ref, res, sem):
+    copies = [pltpu.make_async_copy(lt_ref, t_ref, sem.at[0]), pltpu.make_async_copy(ld_ref, d_ref, sem.at[1])]
+    for copy in copies:
+        copy.start()
+    left = stat_ref[0:4, :]
+    left_ref[...] = left
+    accept_ref[...] = jnp.exp(jnp.minimum(stat_ref[4:8, :], 0.0))
+    scale = 1.0 / jnp.maximum(left, 0.25)
+    for j in range(4):
+        rows = slice(128 * j, 128 * j + 128)
+        col = jnp.broadcast_to(scale[j : j + 1], (128, 128)).T
+        for t in range(4):
+            cols = slice(128 * t, 128 * t + 128)
+            res[rows, cols] = ex_ref[rows, cols] * col
+        copies.append(pltpu.make_async_copy(res.at[rows], r_ref.at[rows], sem.at[2 + j]))
+        copies[-1].start()
+    for copy in copies:
+        copy.wait()
 
 
 def on_device(target_hidden, target_weight, draft_hidden, draft_weight, draft_tokens):
@@ -335,16 +351,17 @@
     n_units = len(UNITS)
     dma = pltpu.SemaphoreType.DMA
     f32 = jnp.float32
-    lt, ld, stat = pl.pallas_call(
+    lt, ld, ex, stat = pl.pallas_call(
         kernel,
         name="verify",
         out_shape=(
-            jax.ShapeDtypeStruct((512, 512), f32),
-            jax.ShapeDtypeStruct((512, 512), f32),
-            jax.ShapeDtypeStruct((16, 128), f32),
+            pltpu.VMEM((512, 512), f32),
+            pltpu.VMEM((512, 512), f32),
+            pltpu.VMEM((512, 512), f32),
+            pltpu.VMEM((8, 128), f32),
         ),
-        in_specs=[anywhere, anywhere, anywhere, anywhere, vmem],
-        out_specs=(anywhere, anywhere, vmem),
+        in_specs=[anywhere] * 5,
+        out_specs=(vmem, vmem, vmem, vmem),
         scratch_shapes=(
             [pltpu.VMEM((2, 4, 4, 2, 16, size), jnp.bfloat16) for _, _, _, size in UNITS]
             + [pltpu.VMEM((2, 2, size, 512), jnp.bfloat16) for _, _, _, size in UNITS]
@@ -355,35 +372,44 @@
                 pltpu.VMEM((2, 512, 512), f32),
                 pltpu.VMEM((512, 512), f32),
                 pltpu.VMEM((512, 512), f32),
+                pltpu.VMEM((4, 128), jnp.int32),
                 pltpu.VMEM((4, 128), f32),
                 pltpu.VMEM((2, 9, 8, 128), f32),
                 pltpu.VMEM((2, 16, 8, 128), f32),
                 dma((n_units, 11)), dma((n_units, 11)),
                 dma((n_units,)), dma((n_units,)), dma((n_units,)),
-                dma((2, 4)), dma((2, 4)), dma((2,)),
-                dma((2,)), dma((2,)),
+                dma((2, 4)), dma((2, 4)), dma((3,)),
+                dma((2, 4)), dma((2, 4)),
                 dma((2, 7)), dma((2,)),
                 dma((2, 15)), dma((2,)),
-                dma((2,)),
             ]
         ),
         compiler_params=pltpu.CompilerParams(
-            collective_id=0, has_side_effects=True, vmem_limit_bytes=56 * 2**20
+            collective_id=0, has_side_effects=True, vmem_limit_bytes=48 * 2**20
         ),
-    )(
-        target_hidden,
-        target_weight.reshape(2, 2, 4096, 512),
-        draft_hidden,
-        draft_weight.reshape(2, 2, 1024, 512),
-        draft_tokens.reshape(4, 128),
-    )
-    t_norm = stat[0:4].reshape(512, 1)
-    d_norm = stat[4:8].reshape(512, 1)
-    leftover = stat[8:12].reshape(512)
-    t_log, d_log = lt - t_norm, ld - d_norm
-    excess = jnp.maximum(jnp.exp(t_log) - jnp.exp(d_log), 0.0)
-    residual = excess / jnp.maximum(leftover, 0.25)[:, None]
-    return t_log, d_log, residual, stat[12:16].reshape(512), leftover
+    )(*[
+        pltpu.with_memory_space_constraint(a, pltpu.HBM)
+        for a in (
+            target_hidden,
+            target_weight.reshape(2, 2, 4096, 512),
+            draft_hidden,
+            draft_weight.reshape(2, 2, 1024, 512),
+            draft_tokens.reshape(4, 128),
+        )
+    ])
+    whole = jax.ShapeDtypeStruct((512, 512), f32)
+    small = jax.ShapeDtypeStruct((4, 128), f32)
+    held = [pltpu.with_memory_space_constraint(a, pltpu.VMEM) for a in (lt, ld, ex, stat)]
+    t_log, d_log, residual, acceptance, leftover = pl.pallas_call(
+        finish,
+        name="finish",
+        out_shape=(whole, whole, whole, small, small),
+        in_specs=[vmem] * 4,
+        out_specs=(anywhere, anywhere, anywhere, vmem, vmem),
+        scratch_shapes=[pltpu.VMEM((512, 512), f32), dma((6,))],
+        compiler_params=pltpu.CompilerParams(vmem_limit_bytes=8 * 2**20),
+    )(*held)
+    return t_log, d_log, residual, acceptance.reshape(512), leftover.reshape(512)
 
 
 def solution(mesh):

time: 99.1 us -> 85.1 us (0.86)
  Pallas kernels: 91.8 us -> 84.3 us
  other arithmetic: 4.82 us -> 0 us
  local copies, waits for them, and re-layouts: 1.34 us -> 0 us
    pallas_call x1 -> x2, Pallas kernels: 91.8 us -> 84.3 us  [the longest x1 82 us: on_device(): pl.pallas_call(kernel, name='verify', out_shape=(pltpu.VMEM((512, 512), f...]
    div x1 -> x0, other arithmetic: 3.56 us -> none  [on_device(): residual = excess / jnp.maximum(leftover, 0.25)[:, None]]
    reshape x1 -> x0, local copies, waits for them, and re-layouts: 1.34 us -> none  [on_device(): return (t_log, d_log, residual, stat[12:16].reshape(512), leftover)]
    max x1 -> x0, other arithmetic: 1.26 us -> none  [on_device(): residual = excess / jnp.maximum(leftover, 0.25)[:, None]]
where the time goes in v2:
time: 85.1 us; the launch traced here: 85 us
  Pallas kernels  84.3 us (99%)
    pallas_call x1, Pallas kernels, on_device(): pl.pallas_call(kernel, name='verify', out_shape=(pltpu.VMEM((512, 512), f...  82 us
    pallas_call x1, Pallas kernels, on_device(): pl.pallas_call(finish, name='finish', out_shape=(whole, whole, whole, sma...  2.29 us

profile of v2, /device:TPU:0, one launch (start us, length us, event | category | flops | bytes accessed | tf_op | source)
XLA Modules:
  0.0 85.0 jit_solution(6733947284243536727)
XLA Ops:
  0.6 82.0 %verify.1 = (f32[512,512]{1,0:T(8,128)S(1)}, f32[512,512]{1,0:T(8,128)S(1)}, f32[512,512]{1,0:T(8,128)S(1)}, f32[8,128]{1,0:T(8,128)S(1)}) custom-call(bf16[4,16384]{1,0:T(4,128)(2,1)} %ht_ref.1, bf16[2,2,4096,512]{3,2,1,0:T(8,128)(2,1)} %bitcast.5, bf16[4,4096]{1,0:T(4,128)(2,1)} %hd_ref.1, bf16[2,2,1024,512]{3,2,1,0:T(8,128)(2,1)} %bitcast.6, s32[4,128]{1,0:T(4,128)} %bitcast.7), custom_call_target="tpu_custom_call" | custom-call | tf_op jit(solution)/shard_map/verify/pallas_call | solution.py:354
  82.7 2.3 %finish.1 = (f32[512,512]{1,0:T(8,128)}, f32[512,512]{1,0:T(8,128)}, f32[512,512]{1,0:T(8,128)}, f32[4,128]{1,0:T(4,128)}, f32[4,128]{1,0:T(4,128)}) custom-call(f32[512,512]{1,0:T(8,128)S(1)} %get-tuple-element.14.lt_ref, f32[512,512]{1,0:T(8,128)S(1)} %get-tuple-element.15.ld_ref, f32[512,512]{1,0:T(8,128)S(1)} %get-tuple-element.16.ex_ref, ...), custom_call_target="tpu_custom_call" | custom-call | tf_op jit(solution)/shard_map/finish/pallas_call | solution.py:403

commit v3 on v2

--- a/solution.py
+++ b/solution.py
@@ -51,8 +51,8 @@
     n_units = len(UNITS)
     hb = scratch[:n_units]
     wb = scratch[n_units : 2 * n_units]
-    (stage_t, stage_d, acc_t, acc_d, part_t, part_d, tok_i, tok_f, near, far,
-     gs, gr, wl, ws, wr, es, er, el, ps, pr, ns, nr, fs, fr) = scratch[2 * n_units :]
+    (hid_t, hid_d, stage_t, stage_d, acc_t, acc_d, part_t, part_d, tok_i, tok_f, tops, near, far,
+     gs, gr, ws, wr, es, er, el, ps, pr, ns, nr, fs, fr) = scratch[2 * n_units :]
     w, n = lax.axis_index("wide"), lax.axis_index("narrow")
     pos = {"x": lax.div(n, 2) * 2 + lax.rem(w, 2), "y": lax.div(w, 8), "z": lax.rem(lax.div(w, 2), 4)}
     c = lax.rem(n, 2)
@@ -75,19 +75,12 @@
     xh, xl = lax.div(pos["x"], 2), lax.rem(pos["x"], 2)
     me = xl * 2 + c
 
-    local = []
-    for u, (order, kind, start, size) in enumerate(UNITS):
-        ref = wt_ref if kind == "t" else wd_ref
-        local.append(pltpu.make_async_copy(ref.at[c, :, pl.ds(start, size), :], wb[u].at[0], wl.at[u]))
-        local[-1].start()
-    own_t = pltpu.make_async_copy(
-        ht_ref.at[:, pl.ds(pl.multiple_of(c * 8192 + xl * 4096, T), 4096)], stage_t.at[me], el.at[0])
-    own_d = pltpu.make_async_copy(
-        hd_ref.at[:, pl.ds(pl.multiple_of(c * 2048 + xl * 1024, T), 1024)], stage_d.at[me], el.at[1])
-    own_tok = pltpu.make_async_copy(tok_ref, tok_i, el.at[2])
-    own_t.start()
-    own_d.start()
-    own_tok.start()
+    got_t = pltpu.make_async_copy(ht_ref, hid_t, el.at[0])
+    got_d = pltpu.make_async_copy(hd_ref, hid_d, el.at[1])
+    got_tok = pltpu.make_async_copy(tok_ref, tok_i, el.at[2])
+    got_d.start()
+    got_t.start()
+    got_tok.start()
 
     steps = (0, 1, 2, 1)
     near_offs = sorted(((a, b) for a in range(4) for b in range(2) if (a, b) != (0, 0)), key=lambda o: -2 * steps[o[0]] - o[1])
@@ -97,6 +90,11 @@
         pl.semaphore_signal(barrier, inc=1, device_id=device(dx=a, dc=b), device_id_type=MESH)
     for a, b in far_offs:
         pl.semaphore_signal(barrier, inc=1, device_id=device(dy=a, dz=b), device_id_type=MESH)
+    for u, (order, kind, start, size) in enumerate(UNITS):
+        ref = wt_ref if kind == "t" else wd_ref
+        pltpu.make_async_copy(ref.at[c, :, pl.ds(start, size), :], wb[u].at[0], wr.at[u]).start()
+    got_d.wait()
+    got_t.wait()
     pl.semaphore_wait(barrier, len(near_offs) + len(far_offs))
 
     swaps = []
@@ -106,10 +104,16 @@
         target = ((pos["y"] * 4 + pos["z"]) * 2 + to_l, xh * 2 + to_c)
         qt = pl.multiple_of(to_c * 8192 + to_l * 4096, T)
         qd = pl.multiple_of(to_c * 2048 + to_l * 1024, T)
-        swaps.append(remote(hd_ref.at[:, pl.ds(qd, 1024)], stage_d.at[me], es.at[1, j], er.at[1, j], target))
-        swaps.append(remote(ht_ref.at[:, pl.ds(qt, 4096)], stage_t.at[me], es.at[0, j], er.at[0, j], target))
+        swaps.append(remote(hid_d.at[:, pl.ds(qd, 1024)], stage_d.at[me], es.at[1, j], er.at[1, j], target))
+        swaps.append(remote(hid_t.at[:, pl.ds(qt, 4096)], stage_t.at[me], es.at[0, j], er.at[0, j], target))
     for s in swaps:
         s.start()
+    own_t = pltpu.make_async_copy(
+        hid_t.at[:, pl.ds(pl.multiple_of(c * 8192 + xl * 4096, T), 4096)], stage_t.at[me], el.at[0])
+    own_d = pltpu.make_async_copy(
+        hid_d.at[:, pl.ds(pl.multiple_of(c * 2048 + xl * 1024, T), 1024)], stage_d.at[me], el.at[1])
+    own_t.start()
+    own_d.start()
     lent = []
     for u, (order, kind, start, size) in enumerate(UNITS):
         ref = wt_ref if kind == "t" else wd_ref
@@ -122,13 +126,22 @@
 
     sends = []
 
-    def send(u, k, src, to):
-        copy = remote(src, src, gs.at[u, k], gr.at[u, k], to)
-        copy.start()
-        sends.append(copy)
-        return copy
-
-    arriving = {}
+    def send(u, phase, src, to):
+        remote(src, src, gs.at[u], gr.at[u, phase], to).start()
+
+    def arrived(u, phase):
+        got = (
+            hb[u].at[0, 0, pl.ds(0, 3), 0],
+            hb[u].at[0, 0],
+            hb[u].at[0, 0, pl.ds(0, 2)],
+            hb[u].at[0],
+            hb[u].at[0, pl.ds(0, 2)],
+        )[phase]
+        remote(got, got, gs.at[u], gr.at[u, phase], partner).wait_recv()
+
+    def sent(u):
+        all63 = part_t.at[pl.ds(0, 504), pl.ds(0, UNITS[u][3])]
+        remote(all63, all63, gs.at[u], gr.at[u, 0], partner).wait_send()
 
     def line(order, c2, part="all"):
         d1, d2, d3 = order
@@ -151,50 +164,44 @@
         rows = [stage[j, :, start : start + size].astype(jnp.float32) for j in range(4)]
         hb[u][xl, pos["y"], pos["z"], xh] = jnp.concatenate(rows, axis=0).astype(jnp.bfloat16)
         mine = hb[u].at[xl, pos["y"], pos["z"], xh]
-        arriving[u, 1] = [send(u, k, mine, shift(order[0], by)) for k, by in ((0, 1), (1, 3), (2, 2))]
-
-    def arrived(u, phase):
-        for copy in arriving[u, phase]:
-            copy.wait_recv()
+        for by in (2, 1, 3):
+            send(u, 0, mine, shift(order[0], by))
 
     def phase2a(u):
         order = ORDERS[UNITS[u][0]]
-        arrived(u, 1)
+        arrived(u, 0)
         mine = hb[u].at[line(order, pos[order[1]])]
-        arriving[u, 2] = [send(u, k, mine, shift(order[1], by)) for k, by in ((3, 1), (4, 3))]
+        for by in (1, 3):
+            send(u, 1, mine, shift(order[1], by))
 
     def phase2b(u):
         order = ORDERS[UNITS[u][0]]
-        arrived(u, 2)
+        arrived(u, 1)
         d = order[1]
-        arriving[u, 3] = [
-            send(u, 5, hb[u].at[line(order, down(d), ("half", 0))], shift(d, 1)),
-            send(u, 6, hb[u].at[line(order, up(d), ("half", 1))], shift(d, 3)),
-        ]
+        send(u, 2, hb[u].at[line(order, down(d), ("half", 0))], shift(d, 1))
+        send(u, 2, hb[u].at[line(order, up(d), ("half", 1))], shift(d, 3))
 
     def phase3a(u):
         order = ORDERS[UNITS[u][0]]
-        arrived(u, 3)
+        arrived(u, 2)
         mine = hb[u].at[plane(order, pos[order[2]])]
-        arriving[u, 4] = [send(u, k, mine, shift(order[2], by)) for k, by in ((7, 1), (8, 3))]
+        for by in (1, 3):
+            send(u, 3, mine, shift(order[2], by))
 
     def phase3b(u):
         order = ORDERS[UNITS[u][0]]
-        arrived(u, 4)
+        arrived(u, 3)
         d = order[2]
-        arriving[u, 5] = [
-            send(u, 9, hb[u].at[plane(order, down(d), ("half", 0))], shift(d, 1)),
-            send(u, 10, hb[u].at[plane(order, up(d), ("half", 1))], shift(d, 3)),
-        ]
+        send(u, 4, hb[u].at[plane(order, down(d), ("half", 0))], shift(d, 1))
+        send(u, 4, hb[u].at[plane(order, up(d), ("half", 1))], shift(d, 3))
 
     begun = set()
 
     def multiply(u, sides=(1, 0), again=False):
         o, kind, start, size = UNITS[u]
         if not again:
-            arrived(u, 5)
-            local[u].wait()
-            lent[u].wait_recv()
+            arrived(u, 4)
+            remote(wb[u], wb[u], ws.at[u], wr.at[u], partner).wait_recv()
         acc = acc_t if kind == "t" else acc_d
         first = kind not in begun
         begun.add(kind)
@@ -237,6 +244,8 @@
             top = jnp.max(most.T, axis=0, keepdims=True)
             top_col = columns(top)
             e = [jnp.exp(t - top_col) for t in tiles]
+            part[rows, :] = jnp.concatenate(e, axis=1)
+            tops[pl.ds(base + j, 1), :] = top
             total = jnp.sum(((e[0] + e[1]) + (e[2] + e[3])).T, axis=0, keepdims=True)
             near[0, 8, pl.ds(base + j, 1), :] = top + jnp.log(total)
             return carry
@@ -248,16 +257,21 @@
 
     def spread(buf, ss, rs, r, me, count, value, targets):
         buf[r, me] = value
-        copies = [remote(buf.at[r, me], buf.at[r, me], ss.at[r, i], rs.at[r], to) for i, to in enumerate(targets)]
-        for copy in copies:
-            copy.start()
-        sends.extend(copies)
+        for to in targets:
+            remote(buf.at[r, me], buf.at[r, me], ss.at[r], rs.at[r], to).start()
+
+    def others(buf, ss, rs, r, count, targets):
         full = buf.at[r, pl.ds(0, count - 1)]
-        remote(full, full, ss.at[r, 0], rs.at[r], targets[0]).wait_recv()
+        return remote(full, full, ss.at[r], rs.at[r], targets[0])
+
+    def gathered(buf, ss, rs, r, count, targets):
+        others(buf, ss, rs, r, count, targets).wait_recv()
         return buf[r, 0:count]
 
     near_to = [device(dx=a, dc=b) for a, b in near_offs]
     far_to = [device(dy=a, dz=b) for a, b in far_offs]
+    near_all = lambda r: (near, ns, nr, r, 8, near_to)
+    far_all = lambda r: (far, fs, fr, r, 16, far_to)
 
     def merge(values):
         top = jnp.max(values, axis=0)
@@ -287,41 +301,68 @@
     every(lambda u: multiply(u, (0,), True), 4)
     totals(1, acc_t, part_t, 0)
 
-    lse = merge(spread(near, ns, nr, 0, near_me, 8, near[0, 8], near_to))
-    lse = merge(spread(far, fs, fr, 0, far_me, 16, lse, far_to))
+    spread(near, ns, nr, 0, near_me, 8, near[0, 8], near_to)
+    got_tok.wait()
+    tok_f[...] = (tok_i[...] - (w * 4 + n) * 512).astype(jnp.float32)
+
+    def pick(j, carry):
+        rows = pl.ds(pl.multiple_of(j * 128, 128), 128)
+        tok = columns(tok_f[pl.ds(j, 1), :])
+        lanes = lax.broadcasted_iota(jnp.int32, (128, 128), 1).astype(jnp.float32)
+        picked = None
+        for t in range(4):
+            cols = slice(128 * t, 128 * t + 128)
+            p = jnp.where(tok == lanes + 128.0 * t, acc_t[0, rows, cols] - acc_d[0, rows, cols], 0.0)
+            picked = p if picked is None else picked + p
+        near[1, 8, pl.ds(4 + j, 1), :] = jnp.sum(picked.T, axis=0, keepdims=True)
+        return carry
+
+    lax.fori_loop(0, 4, pick, 0)
+    lse = merge(gathered(*near_all(0)))
+    spread(far, fs, fr, 0, far_me, 16, lse, far_to)
+    lse = merge(gathered(*far_all(0)))
     near[0, 8] = lse
-
-    own_tok.wait()
-    offset = (w * 4 + n) * 512
-    tok_f[...] = (tok_i[...] - offset).astype(jnp.float32)
+    tops[...] = jnp.exp(tops[...] - lse)
 
     def mass(j, carry):
         rows = pl.ds(pl.multiple_of(j * 128, 128), 128)
-        lt, ld = acc_t[0, rows, :], acc_d[0, rows, :]
+        t_col = columns(tops[pl.ds(j, 1), :])
+        d_col = columns(tops[pl.ds(4 + j, 1), :])
+        kept = None
+        for t in range(4):
+            cols = slice(128 * t, 128 * t + 128)
+            e = jnp.maximum(part_t[rows, cols] * t_col - part_d[rows, cols] * d_col, 0.0)
+            ex_ref[rows, cols] = e
+            kept = e if kept is None else kept + e
+        near[1, 8, pl.ds(j, 1), :] = jnp.sum(kept.T, axis=0, keepdims=True)
+        return carry
+
+    lax.fori_loop(0, 4, mass, 0)
+
+    spread(near, ns, nr, 1, near_me, 8, near[1, 8], near_to)
+
+    def normalize(j, carry):
+        rows = pl.ds(pl.multiple_of(j * 128, 128), 128)
         t_col = columns(near[0, 8, pl.ds(j, 1), :])
         d_col = columns(near[0, 8, pl.ds(4 + j, 1), :])
-        tok = columns(tok_f[pl.ds(j, 1), :])
-        lanes = lax.broadcasted_iota(jnp.int32, (128, 128), 1).astype(jnp.float32)
-        kept, picked = None, None
         for t in range(4):
-            lp = lt[:, 128 * t : 128 * t + 128] - t_col
-            dp = ld[:, 128 * t : 128 * t + 128] - d_col
-            lt_ref[rows, 128 * t : 128 * t + 128] = lp
-            ld_ref[rows, 128 * t : 128 * t + 128] = dp
-            e = jnp.maximum(jnp.exp(lp) - jnp.exp(dp), 0.0)
-            ex_ref[rows, 128 * t : 128 * t + 128] = e
-            p = jnp.where(tok == lanes + 128.0 * t, lp - dp, 0.0)
-            kept = e if kept is None else kept + e
-            picked = p if picked is None else picked + p
-        near[1, 8, pl.ds(j, 1), :] = jnp.sum(kept.T, axis=0, keepdims=True)
-        near[1, 8, pl.ds(4 + j, 1), :] = jnp.sum(picked.T, axis=0, keepdims=True)
+            cols = slice(128 * t, 128 * t + 128)
+            lt_ref[rows, cols] = acc_t[0, rows, cols] - t_col
+            ld_ref[rows, cols] = acc_d[0, rows, cols] - d_col
         return carry
 
-    lax.fori_loop(0, 4, mass, 0)
-    both = jnp.sum(spread(near, ns, nr, 1, near_me, 8, near[1, 8], near_to), axis=0)
-    both = jnp.sum(spread(far, fs, fr, 1, far_me, 16, both, far_to), axis=0)
-    stat_ref[...] = both
-
+    lax.fori_loop(0, 4, normalize, 0)
+    both = jnp.sum(gathered(*near_all(1)), axis=0)
+    spread(far, fs, fr, 1, far_me, 16, both, far_to)
+    both = jnp.sum(gathered(*far_all(1)), axis=0)
+    stat_ref[0:4, :] = both[0:4]
+    stat_ref[4:8, :] = both[4:8] - (lse[0:4] - lse[4:8])
+
+    for r in range(2):
+        others(*near_all(r)).wait_send()
+        others(*far_all(r)).wait_send()
+    for u in range(n_units):
+        sent(u)
     for s in swaps + lent + sends:
         s.wait_send()
 
@@ -366,6 +407,8 @@
             [pltpu.VMEM((2, 4, 4, 2, 16, size), jnp.bfloat16) for _, _, _, size in UNITS]
             + [pltpu.VMEM((2, 2, size, 512), jnp.bfloat16) for _, _, _, size in UNITS]
             + [
+                pltpu.VMEM((4, 16384), jnp.bfloat16),
+                pltpu.VMEM((4, 4096), jnp.bfloat16),
                 pltpu.VMEM((4, 4, 4096), jnp.bfloat16),
                 pltpu.VMEM((4, 4, 1024), jnp.bfloat16),
                 pltpu.VMEM((2, 512, 512), f32),
@@ -374,14 +417,15 @@
                 pltpu.VMEM((512, 512), f32),
                 pltpu.VMEM((4, 128), jnp.int32),
                 pltpu.VMEM((4, 128), f32),
+                pltpu.VMEM((8, 128), f32),
                 pltpu.VMEM((2, 9, 8, 128), f32),
                 pltpu.VMEM((2, 16, 8, 128), f32),
-                dma((n_units, 11)), dma((n_units, 11)),
-                dma((n_units,)), dma((n_units,)), dma((n_units,)),
+                dma((n_units,)), dma((n_units, 5)),
+                dma((n_units,)), dma((n_units,)),
                 dma((2, 4)), dma((2, 4)), dma((3,)),
                 dma((2, 4)), dma((2, 4)),
-                dma((2, 7)), dma((2,)),
-                dma((2, 15)), dma((2,)),
+                dma((2,)), dma((2,)),
+                dma((2,)), dma((2,)),
             ]
         ),
         compiler_params=pltpu.CompilerParams(

time: 85.1 us -> 81 us (0.952)
  Pallas kernels: 84.3 us -> 80.3 us
    pallas_call x1, Pallas kernels: 82 us -> 78 us  [on_device(): pl.pallas_call(kernel, name='verify', out_shape=(pltpu.VMEM((512, 512), f...]
where the time goes in v3:
time: 81 us; the launch traced here: 80.9 us
  Pallas kernels  80.3 us (99%)
    pallas_call x1, Pallas kernels, on_device(): pl.pallas_call(kernel, name='verify', out_shape=(pltpu.VMEM((512, 512), f...  78 us
    pallas_call x1, Pallas kernels, on_device(): pl.pallas_call(finish, name='finish', out_shape=(whole, whole, whole, sma...  2.29 us

profile of v3, /device:TPU:0, one launch (start us, length us, event | category | flops | bytes accessed | tf_op | source)
XLA Modules:
  0.0 80.9 jit_solution(8210846076536947970)
XLA Ops:
  0.6 78.0 %verify.1 = (f32[512,512]{1,0:T(8,128)S(1)}, f32[512,512]{1,0:T(8,128)S(1)}, f32[512,512]{1,0:T(8,128)S(1)}, f32[8,128]{1,0:T(8,128)S(1)}) custom-call(bf16[4,16384]{1,0:T(4,128)(2,1)} %ht_ref.1, bf16[2,2,4096,512]{3,2,1,0:T(8,128)(2,1)} %bitcast.5, bf16[4,4096]{1,0:T(4,128)(2,1)} %hd_ref.1, bf16[2,2,1024,512]{3,2,1,0:T(8,128)(2,1)} %bitcast.6, s32[4,128]{1,0:T(4,128)} %bitcast.7), custom_call_target="tpu_custom_call" | custom-call | tf_op jit(solution)/shard_map/verify/pallas_call | solution.py:395
  78.6 2.3 %finish.1 = (f32[512,512]{1,0:T(8,128)}, f32[512,512]{1,0:T(8,128)}, f32[512,512]{1,0:T(8,128)}, f32[4,128]{1,0:T(4,128)}, f32[4,128]{1,0:T(4,128)}) custom-call(f32[512,512]{1,0:T(8,128)S(1)} %get-tuple-element.14.lt_ref, f32[512,512]{1,0:T(8,128)S(1)} %get-tuple-element.15.ld_ref, f32[512,512]{1,0:T(8,128)S(1)} %get-tuple-element.16.ex_ref, ...), custom_call_target="tpu_custom_call" | custom-call | tf_op jit(solution)/shard_map/finish/pallas_call | solution.py:447

commit v4 on v3

--- a/solution.py
+++ b/solution.py
@@ -86,16 +86,15 @@
     near_offs = sorted(((a, b) for a in range(4) for b in range(2) if (a, b) != (0, 0)), key=lambda o: -2 * steps[o[0]] - o[1])
     far_offs = sorted(((a, b) for a in range(4) for b in range(4) if (a, b) != (0, 0)), key=lambda o: -steps[o[0]] - steps[o[1]])
     barrier = pltpu.get_barrier_semaphore()
-    for a, b in near_offs:
-        pl.semaphore_signal(barrier, inc=1, device_id=device(dx=a, dc=b), device_id_type=MESH)
-    for a, b in far_offs:
-        pl.semaphore_signal(barrier, inc=1, device_id=device(dy=a, dz=b), device_id_type=MESH)
+    greeted = [device(**{"d" + d: by}) for by in (2, 1, 3) for d in "xyz"] + [partner, (w + 1 - 2 * xl, xh * 2 + 1 - c)]
+    for to in greeted:
+        pl.semaphore_signal(barrier, inc=1, device_id=to, device_id_type=MESH)
     for u, (order, kind, start, size) in enumerate(UNITS):
         ref = wt_ref if kind == "t" else wd_ref
         pltpu.make_async_copy(ref.at[c, :, pl.ds(start, size), :], wb[u].at[0], wr.at[u]).start()
     got_d.wait()
     got_t.wait()
-    pl.semaphore_wait(barrier, len(near_offs) + len(far_offs))
+    pl.semaphore_wait(barrier, len(greeted))
 
     swaps = []
     for j in range(1, 4):
@@ -295,9 +294,10 @@
     totals(0, acc_d, part_d, 4)
     every(phase3b, 4)
     every(multiply, 2)
-    every(multiply, 3)
+    every(lambda u: multiply(u, (1,)), 3)
     every(lambda u: multiply(u, (1,)), 4)
     give(1, acc_t, part_t)
+    every(lambda u: multiply(u, (0,), True), 3)
     every(lambda u: multiply(u, (0,), True), 4)
     totals(1, acc_t, part_t, 0)
 

time: 81 us -> 79.7 us (0.984)
  Pallas kernels: 80.3 us -> 78.9 us
    pallas_call x1, Pallas kernels: 78 us -> 76.6 us  [on_device(): pl.pallas_call(kernel, name='verify', out_shape=(pltpu.VMEM((512, 512), f...]
where the time goes in v4:
time: 79.7 us; the launch traced here: 79.5 us
  Pallas kernels  78.9 us (99%)
    pallas_call x1, Pallas kernels, on_device(): pl.pallas_call(kernel, name='verify', out_shape=(pltpu.VMEM((512, 512), f...  76.6 us
    pallas_call x1, Pallas kernels, on_device(): pl.pallas_call(finish, name='finish', out_shape=(whole, whole, whole, sma...  2.29 us

profile of v4, /device:TPU:0, one launch (start us, length us, event | category | flops | bytes accessed | tf_op | source)
XLA Modules:
  0.0 79.5 jit_solution(11719710945203527645)
XLA Ops:
  0.6 76.6 %verify.1 = (f32[512,512]{1,0:T(8,128)S(1)}, f32[512,512]{1,0:T(8,128)S(1)}, f32[512,512]{1,0:T(8,128)S(1)}, f32[8,128]{1,0:T(8,128)S(1)}) custom-call(bf16[4,16384]{1,0:T(4,128)(2,1)} %ht_ref.1, bf16[2,2,4096,512]{3,2,1,0:T(8,128)(2,1)} %bitcast.5, bf16[4,4096]{1,0:T(4,128)(2,1)} %hd_ref.1, bf16[2,2,1024,512]{3,2,1,0:T(8,128)(2,1)} %bitcast.6, s32[4,128]{1,0:T(4,128)} %bitcast.7), custom_call_target="tpu_custom_call" | custom-call | tf_op jit(solution)/shard_map/verify/pallas_call | solution.py:395
  77.3 2.3 %finish.1 = (f32[512,512]{1,0:T(8,128)}, f32[512,512]{1,0:T(8,128)}, f32[512,512]{1,0:T(8,128)}, f32[4,128]{1,0:T(4,128)}, f32[4,128]{1,0:T(4,128)}) custom-call(f32[512,512]{1,0:T(8,128)S(1)} %get-tuple-element.14.lt_ref, f32[512,512]{1,0:T(8,128)S(1)} %get-tuple-element.15.ld_ref, f32[512,512]{1,0:T(8,128)S(1)} %get-tuple-element.16.ex_ref, ...), custom_call_target="tpu_custom_call" | custom-call | tf_op jit(solution)/shard_map/finish/pallas_call | solution.py:447

commit v5 on v4

--- a/solution.py
+++ b/solution.py
@@ -103,7 +103,7 @@
         target = ((pos["y"] * 4 + pos["z"]) * 2 + to_l, xh * 2 + to_c)
         qt = pl.multiple_of(to_c * 8192 + to_l * 4096, T)
         qd = pl.multiple_of(to_c * 2048 + to_l * 1024, T)
-        swaps.append(remote(hid_d.at[:, pl.ds(qd, 1024)], stage_d.at[me], es.at[1, j], er.at[1, j], target))
+        swaps.insert(j - 1, remote(hid_d.at[:, pl.ds(qd, 1024)], stage_d.at[me], es.at[1, j], er.at[1, j], target))
         swaps.append(remote(hid_t.at[:, pl.ds(qt, 4096)], stage_t.at[me], es.at[0, j], er.at[0, j], target))
     for s in swaps:
         s.start()
@@ -118,10 +118,7 @@
         ref = wt_ref if kind == "t" else wd_ref
         lent.append(remote(ref.at[1 - c, :, pl.ds(start, size), :], wb[u].at[1], ws.at[u], wr.at[u], partner))
         lent[-1].start()
-    own_t.wait()
-    own_d.wait()
-    for s in swaps:
-        s.wait_recv()
+    swaps_d, swaps_t = swaps[:3], swaps[3:]
 
     sends = []
 
@@ -276,7 +273,16 @@
         top = jnp.max(values, axis=0)
         return top + jnp.log(jnp.sum(jnp.exp(values - top[None]), axis=0))
 
-    for phase in (phase1, phase2a, phase2b):
+    own_d.wait()
+    for s in swaps_d:
+        s.wait_recv()
+    every(phase1, 0)
+    own_t.wait()
+    for s in swaps_t:
+        s.wait_recv()
+    for g in range(1, GROUPS):
+        every(phase1, g)
+    for phase in (phase2a, phase2b):
         for g in range(GROUPS):
             every(phase, g)
     every(phase3a, 0)
@@ -352,19 +358,20 @@
         return carry
 
     lax.fori_loop(0, 4, normalize, 0)
+    for u in range(n_units):
+        sent(u)
+    for s in swaps + lent + sends:
+        s.wait_send()
+    others(*near_all(0)).wait_send()
+    others(*far_all(0)).wait_send()
     both = jnp.sum(gathered(*near_all(1)), axis=0)
     spread(far, fs, fr, 1, far_me, 16, both, far_to)
     both = jnp.sum(gathered(*far_all(1)), axis=0)
     stat_ref[0:4, :] = both[0:4]
     stat_ref[4:8, :] = both[4:8] - (lse[0:4] - lse[4:8])
 
-    for r in range(2):
-        others(*near_all(r)).wait_send()
-        others(*far_all(r)).wait_send()
-    for u in range(n_units):
-        sent(u)
-    for s in swaps + lent + sends:
-        s.wait_send()
+    others(*near_all(1)).wait_send()
+    others(*far_all(1)).wait_send()
 
 
 def finish(lt_ref, ld_ref, ex_ref, stat_ref, t_ref, d_ref, r_ref, accept_ref, left_ref, res, sem):

time: 79.7 us -> 79.1 us (level)
  no operation moved by 1% of the time
where the time goes in v5:
time: 79.1 us; the launch traced here: 79 us
  Pallas kernels  78.4 us (99%)
    pallas_call x1, Pallas kernels, on_device(): pl.pallas_call(kernel, name='verify', out_shape=(pltpu.VMEM((512, 512), f...  76.1 us
    pallas_call x1, Pallas kernels, on_device(): pl.pallas_call(finish, name='finish', out_shape=(whole, whole, whole, sma...  2.29 us

profile of v5, /device:TPU:0, one launch (start us, length us, event | category | flops | bytes accessed | tf_op | source)
XLA Modules:
  0.0 79.0 jit_solution(14230311320358217457)
XLA Ops:
  0.6 76.1 %verify.1 = (f32[512,512]{1,0:T(8,128)S(1)}, f32[512,512]{1,0:T(8,128)S(1)}, f32[512,512]{1,0:T(8,128)S(1)}, f32[8,128]{1,0:T(8,128)S(1)}) custom-call(bf16[4,16384]{1,0:T(4,128)(2,1)} %ht_ref.1, bf16[2,2,4096,512]{3,2,1,0:T(8,128)(2,1)} %bitcast.5, bf16[4,4096]{1,0:T(4,128)(2,1)} %hd_ref.1, bf16[2,2,1024,512]{3,2,1,0:T(8,128)(2,1)} %bitcast.6, s32[4,128]{1,0:T(4,128)} %bitcast.7), custom_call_target="tpu_custom_call" | custom-call | tf_op jit(solution)/shard_map/verify/pallas_call | solution.py:402
  76.7 2.3 %finish.1 = (f32[512,512]{1,0:T(8,128)}, f32[512,512]{1,0:T(8,128)}, f32[512,512]{1,0:T(8,128)}, f32[4,128]{1,0:T(4,128)}, f32[4,128]{1,0:T(4,128)}) custom-call(f32[512,512]{1,0:T(8,128)S(1)} %get-tuple-element.14.lt_ref, f32[512,512]{1,0:T(8,128)S(1)} %get-tuple-element.15.ld_ref, f32[512,512]{1,0:T(8,128)S(1)} %get-tuple-element.16.ex_ref, ...), custom_call_target="tpu_custom_call" | custom-call | tf_op jit(solution)/shard_map/finish/pallas_call | solution.py:454

commit v6 on v5

--- a/solution.py
+++ b/solution.py
@@ -295,11 +295,15 @@
     give(0, acc_d, part_d)
     every(phase3b, 2)
     every(phase3a, 4)
-    every(multiply, 1)
+    multiply(3)
+    multiply(4)
     every(phase3b, 3)
+    multiply(5)
     totals(0, acc_d, part_d, 4)
+    multiply(6)
     every(phase3b, 4)
-    every(multiply, 2)
+    multiply(7)
+    multiply(8)
     every(lambda u: multiply(u, (1,)), 3)
     every(lambda u: multiply(u, (1,)), 4)
     give(1, acc_t, part_t)

time: 79.1 us -> 78.9 us (level)
  no operation moved by 1% of the time
where the time goes in v6:
time: 78.9 us; the launch traced here: 78.8 us
  Pallas kernels  78.2 us (99%)
    pallas_call x1, Pallas kernels, on_device(): pl.pallas_call(kernel, name='verify', out_shape=(pltpu.VMEM((512, 512), f...  75.9 us
    pallas_call x1, Pallas kernels, on_device(): pl.pallas_call(finish, name='finish', out_shape=(whole, whole, whole, sma...  2.29 us

profile of v6, /device:TPU:0, one launch (start us, length us, event | category | flops | bytes accessed | tf_op | source)
XLA Modules:
  0.0 78.8 jit_solution(4465075970615156078)
XLA Ops:
  0.6 75.9 %verify.1 = (f32[512,512]{1,0:T(8,128)S(1)}, f32[512,512]{1,0:T(8,128)S(1)}, f32[512,512]{1,0:T(8,128)S(1)}, f32[8,128]{1,0:T(8,128)S(1)}) custom-call(bf16[4,16384]{1,0:T(4,128)(2,1)} %ht_ref.1, bf16[2,2,4096,512]{3,2,1,0:T(8,128)(2,1)} %bitcast.5, bf16[4,4096]{1,0:T(4,128)(2,1)} %hd_ref.1, bf16[2,2,1024,512]{3,2,1,0:T(8,128)(2,1)} %bitcast.6, s32[4,128]{1,0:T(4,128)} %bitcast.7), custom_call_target="tpu_custom_call" | custom-call | tf_op jit(solution)/shard_map/verify/pallas_call | solution.py:406
  76.5 2.3 %finish.1 = (f32[512,512]{1,0:T(8,128)}, f32[512,512]{1,0:T(8,128)}, f32[512,512]{1,0:T(8,128)}, f32[4,128]{1,0:T(4,128)}, f32[4,128]{1,0:T(4,128)}) custom-call(f32[512,512]{1,0:T(8,128)S(1)} %get-tuple-element.14.lt_ref, f32[512,512]{1,0:T(8,128)S(1)} %get-tuple-element.15.ld_ref, f32[512,512]{1,0:T(8,128)S(1)} %get-tuple-element.16.ex_ref, ...), custom_call_target="tpu_custom_call" | custom-call | tf_op jit(solution)/shard_map/finish/pallas_call | solution.py:458
